TPU v7x, 32 devices: a whole 2x2x4 slice. The times are simulated.
32 devices in a mesh: shot: 4 (over y, core), cmp: 8 (over z, x).
Axes of the slice: x: 2, y: 2, z: 4, core: 2. Of those that a mesh axis runs over, the one named last changes fastest.
Arguments:
- traces: float32 [8192, 1024], P(('shot', 'cmp')), may hold values from -6 to 6
- offsets: int32 [8192], P(('shot', 'cmp')), may hold values from 0 to 64
- cmp_bin: int32 [8192, 1], P(('shot', 'cmp')), may hold values from 0 to 255; in each aligned block of 256 rows (0 to 255, 256 to 511, ...) at most 2 rows name the same one
- shot_slot: int32 [8192], P(('shot', 'cmp')), may hold values from 0 to 7
- receiver_id: int32 [8192], P(('shot', 'cmp')), may hold values from 0 to 511
- band: float32 [8, 1024], replicated, may hold values from -2 to 2
Outputs:
- shot_corr: float32 [256, 128], P(('shot', 'cmp'))
- recv_corr: float32 [512, 128], P(('shot', 'cmp'))
Inputs may be any that keep to these rules, and one draw needn't show every extreme that they name: `cmp_bin`: among the rows of one device, no bin is named more than 2 times, a bound that some block reaches; every bin is named by some trace.
All inputs are finite; a program needn't handle non-finite values.
Results may differ from a plain program's by a relative error of at most 0.000068.
Values sent between devices are 32-bit elements; how exact they have to be, the bound alone decides.
A program may use at most 64 MiB of HBM per device.

v0:
```python
import jax
import jax.numpy as jnp
from jax import lax
from jax.sharding import PartitionSpec as P

LAGS = 128
MAXOFF = 64
SLOT = 2
SHOT_DEV = 8
RECV_DEV = 16


def moveout(block, shifts, band):
    width = block.shape[1]
    taps = band.shape[0]
    extra = (MAXOFF + taps + 127) // 128 * 128
    current = jnp.pad(block, ((0, 0), (0, extra)))
    levels = max(MAXOFF.bit_length(), 1)
    for level in range(levels):
        step = 1 << level
        moved = jnp.pad(current[:, step:], ((0, 0), (0, step)))
        chosen = (shifts >> level & 1)[:, None] == 1
        current = jnp.where(chosen, moved, current)
    total = jnp.zeros((block.shape[0], width), jnp.float32)
    for tap_index in range(taps):
        total = total + band[tap_index][None, :] * current[:, tap_index : tap_index + width]
    return total


def lag_table(padded, samples):
    return jnp.stack(
        [padded[..., lag_index : lag_index + samples] for lag_index in range(LAGS)], axis=-1
    )


def correlate(arrived, markers):
    samples = arrived.shape[-1]
    fold = jnp.sum(markers, axis=(0, 2))
    pilot = jnp.sum(arrived, axis=(0, 2)) / fold[:, None]
    half = LAGS // 2
    padded = jnp.pad(pilot, ((0, 0), (half, LAGS - half)))
    toeplitz = lag_table(padded, samples)
    corr = jnp.einsum(
        "dbsn,bnl->dbsl",
        arrived,
        toeplitz,
        precision=lax.Precision.HIGHEST,
        preferred_element_type=jnp.float32,
    )
    return corr * (1.0 / samples)


def local(traces, offsets, cmp_bin, shot_slot, receiver_id, band):
    rows, samples = traces.shape
    devices = lax.axis_size(("shot", "cmp"))
    corrected = moveout(traces, offsets, band)
    bins = cmp_bin[:, 0]
    bins_here = rows // devices
    same_bin = bins[:, None] == bins[None, :]
    earlier = lax.broadcasted_iota(jnp.int32, (rows, rows), 1) < lax.broadcasted_iota(
        jnp.int32, (rows, rows), 0
    )
    ranks = jnp.sum(jnp.logical_and(same_bin, earlier).astype(jnp.int32), axis=1)
    places = bins * SLOT + ranks
    total_slots = bins_here * devices * SLOT
    place_table = (
        places[None, :] == lax.broadcasted_iota(jnp.int32, (total_slots, rows), 0)
    ).astype(jnp.float32)
    back_table = (
        places[:, None] == lax.broadcasted_iota(jnp.int32, (rows, total_slots), 1)
    ).astype(jnp.float32)
    outgoing = jnp.dot(
        place_table, corrected, precision=lax.Precision.HIGHEST, preferred_element_type=jnp.float32
    )
    markers = jnp.sum(place_table, axis=1)
    outgoing = outgoing.reshape(devices, bins_here, SLOT, samples)
    markers = markers.reshape(devices, bins_here, SLOT)
    returned = lax.all_to_all(
        correlate(
            lax.all_to_all(outgoing, ("shot", "cmp"), split_axis=0, concat_axis=0, tiled=True),
            lax.all_to_all(markers, ("shot", "cmp"), split_axis=0, concat_axis=0, tiled=True),
        ),
        ("shot", "cmp"),
        split_axis=0,
        concat_axis=0,
        tiled=True,
    )
    corr_traces = jnp.dot(
        back_table,
        returned.reshape(total_slots, LAGS),
        precision=lax.Precision.HIGHEST,
        preferred_element_type=jnp.float32,
    )
    shot_table = (
        shot_slot[None, :] == lax.broadcasted_iota(jnp.int32, (SHOT_DEV, rows), 0)
    ).astype(jnp.float32)
    shot_corr = jnp.dot(
        shot_table, corr_traces, precision=lax.Precision.HIGHEST, preferred_element_type=jnp.float32
    )
    wanted = lax.broadcasted_iota(jnp.int32, (RECV_DEV * lax.axis_size(("shot", "cmp")), rows), 0)
    table = (receiver_id[None, :] == wanted).astype(jnp.float32)
    recv_corr = lax.psum_scatter(
        jnp.dot(
            table, corr_traces, precision=lax.Precision.HIGHEST, preferred_element_type=jnp.float32
        ),
        ("shot", "cmp"),
        scatter_dimension=0,
        tiled=True,
    )
    return (shot_corr, recv_corr)


def solution(mesh):
    placed = (
        P(("shot", "cmp"), None),
        P(("shot", "cmp")),
        P(("shot", "cmp"), None),
        P(("shot", "cmp")),
        P(("shot", "cmp")),
        P(),
    )
    return jax.shard_map(
        local,
        mesh=mesh,
        in_specs=placed,
        out_specs=(P(("shot", "cmp"), None), P(("shot", "cmp"), None)),
        check_vma=False,
    )
```

profile of v0, /device:TPU:0, one launch (start us, length us, event | category | flops | bytes accessed | tf_op | source)
XLA Modules:
  0.0 260.6 jit_solution(7819935108088552357)
XLA Ops:
  7.2 0.9 convert_reduce_fusion.1
  8.1 0.7 multiply_add_fusion
  9.1 0.9 copy.4398
  9.9 7.3 %all-to-all-start.1 = ((f32[32,8,2]{1,2,0:T(2,128)}), f32[32,8,2]{1,2,0:T(2,128)S(1)}, u32[]{:S(2)}, u32[]{:S(2)}) async-start(f32[32,8,2]{1,2,0:T(2,128)} %copy.4398), calls=%async_computation.1 | async-start | bytes 65536 | tf_op jit(solution)/shard_map/all_to_all | solution.py:81
  17.2 0.7 and_compare_fusion.6
  17.9 1.1 fusion.44
  19.0 1.6 pad_slice_fusion
  20.6 1.4 pad_select_fusion.6
  22.0 0.4 slice.601
  22.4 0.2 pad_select_fusion.5
  22.6 0.4 slice.602
  23.0 0.2 pad_select_fusion.4
  23.2 0.4 slice.603
  23.6 0.2 pad_select_fusion.3
  23.8 0.4 slice.604
  24.2 0.2 pad_select_fusion.2
  24.4 0.4 slice.605
  25.0 0.4 slice.606
  25.3 0.2 pad_select_fusion
  25.6 2.9 %fusion.14 = f32[512,1024]{1,0:T(8,128)S(1)} fusion(f32[256,1152]{1,0:T(8,128)S(1)} %pad_select_fusion, f32[1024]{0:T(1024)S(1)} %bitcast.288, f32[1024]{0:T(1024)S(1)} %bitcast.289, f32[1024]{0:T(1024)S(1)} %bitcast.283, f32[1024]{0:T(1024)S(1)} %bitcast.284, f32[1024]{0:T(1024)S(1)} %bitcast.285, f32[1024]{0:T(1024)S(1)} %bitcast.286, ...), kind=kOutput, calls=%fused_computation.15 | convolution fusion | flops 1614675968 | bytes 10519552 | tf_op jit(solution)/shard_map/dot_general | solution.py:72
  28.5 2.3 reshape.67
  30.8 6.0 %all-to-all-start = ((f32[32,8,2,1024]{3,2,1,0:T(2,128)}), f32[32,8,2,1024]{3,2,1,0:T(2,128)S(1)}, u32[]{:S(2)}, u32[]{:S(2)}) async-start(f32[32,8,2,1024]{3,2,1,0:T(2,128)} %reshape.67), calls=%async_computation | async-start | bytes 4194304 | tf_op jit(solution)/shard_map/all_to_all | solution.py:80
  36.8 49.8 %all-to-all-done = f32[32,8,2,1024]{3,2,1,0:T(2,128)S(1)} async-done(((f32[32,8,2,1024]{3,2,1,0:T(2,128)}), f32[32,8,2,1024]{3,2,1,0:T(2,128)S(1)}, u32[]{:S(2)}, u32[]{:S(2)}) %all-to-all-start) | async-done | bytes 2097184 | tf_op jit(solution)/shard_map/all_to_all | solution.py:80
  86.7 0.7 reduce_sum.42
  97.5 8.2 %fusion.8 = f32[32,8,2,128]{3,0,2,1:T(8,128)S(1)} fusion(f32[32,8,2,1024]{3,2,1,0:T(2,128)S(1)} %all-to-all-done, f32[8,1024,128,1]{1,0,2,3:T(8,128)S(1)} %bitcast.276), kind=kOutput, calls=%fused_computation.12 | convolution fusion | flops 805371904 | bytes 6553600 | tf_op jit(solution)/shard_map/dbsn,bnl->dbsl/dot_general | solution.py:43
  105.7 0.9 copy.4401
  106.6 3.2 %all-to-all-start.2 = ((f32[32,8,2,128]{3,2,1,0:T(2,128)}), f32[32,8,2,128]{3,2,1,0:T(2,128)S(1)}, u32[]{:S(2)}, u32[]{:S(2)}) async-start(f32[32,8,2,128]{3,2,1,0:T(2,128)} %copy.4401), calls=%async_computation.2 | async-start | bytes 524288 | tf_op jit(solution)/shard_map/all_to_all | solution.py:78
  109.9 10.6 %all-to-all-done.2 = f32[32,8,2,128]{3,2,1,0:T(2,128)S(1)} async-done(((f32[32,8,2,128]{3,2,1,0:T(2,128)}), f32[32,8,2,128]{3,2,1,0:T(2,128)S(1)}, u32[]{:S(2)}, u32[]{:S(2)}) %all-to-all-start.2) | async-done | bytes 262176 | tf_op jit(solution)/shard_map/all_to_all | solution.py:78
  120.5 0.4 fusion.36
  120.9 1.1 fusion.37
  122.0 0.8 fusion.42
  122.8 131.0 %reduce-scatter.2.cloned.1.call-done = f32[16,128]{1,0:T(8,128)} async-done(((f32[512,128]{1,0:T(8,128)}), f32[16,128]{1,0:T(8,128)}) %reduce-scatter.2.cloned.1.call-update) | async-done | bytes 8208 | tf_op jit(solution)/shard_map/reduce_scatter | solution.py:102
  (143 shorter events, 10.6 us)
Async XLA Ops:
  9.9 20.8 %all-to-all-start.1 = ((f32[32,8,2]{1,2,0:T(2,128)}), f32[32,8,2]{1,2,0:T(2,128)S(1)}, u32[]{:S(2)}, u32[]{:S(2)}) async-start(f32[32,8,2]{1,2,0:T(2,128)} %copy.4398), calls=%async_computation.1 | async-start | bytes 65536 | tf_op jit(solution)/shard_map/all_to_all | solution.py:81
  30.8 55.9 %all-to-all-start = ((f32[32,8,2,1024]{3,2,1,0:T(2,128)}), f32[32,8,2,1024]{3,2,1,0:T(2,128)S(1)}, u32[]{:S(2)}, u32[]{:S(2)}) async-start(f32[32,8,2,1024]{3,2,1,0:T(2,128)} %reshape.67), calls=%async_computation | async-start | bytes 4194304 | tf_op jit(solution)/shard_map/all_to_all | solution.py:80
  97.5 12.4 %copy-start = (s32[256,1]{0,1:T(1,128)S(1)}, s32[256,1]{0,1:T(1,128)}, u32[]{:S(2)}) copy-start(s32[256,1]{0,1:T(1,128)} %param.8) | copy-start | bytes 3076
  97.5 23.4 %copy-start.1 = (s32[256]{0:T(256)S(1)}, s32[256]{0:T(256)}, u32[]{:S(2)}) copy-start(s32[256]{0:T(256)} %param.10) | copy-start | bytes 3076
  97.5 24.5 %copy-start.2 = (s32[256]{0:T(256)S(1)}, s32[256]{0:T(256)}, u32[]{:S(2)}) copy-start(s32[256]{0:T(256)} %param.9) | copy-start | bytes 3076
  106.6 13.9 %all-to-all-start.2 = ((f32[32,8,2,128]{3,2,1,0:T(2,128)}), f32[32,8,2,128]{3,2,1,0:T(2,128)S(1)}, u32[]{:S(2)}, u32[]{:S(2)}) async-start(f32[32,8,2,128]{3,2,1,0:T(2,128)} %copy.4401), calls=%async_computation.2 | async-start | bytes 524288 | tf_op jit(solution)/shard_map/all_to_all | solution.py:78
  109.8 143.9 %reduce-scatter.2.cloned.1.call-start = ((), (), s32[]{:S(2)}) async-start(), calls=%async_computation.4 | async-start | bytes 270336 | tf_op jit(solution)/shard_map/reduce_scatter | solution.py:102
Sparse Core Ops, SparseCore 0:
  122.1 131.5 reduce-scatter.1
where the time goes:
time: 261 us
  waiting for transfers between devices  191 us (73%)
  local copies, waits for them, and re-layouts  19 us (7%)
  starting transfers between devices  16.6 us (6%)
  between operations  14.3 us (5%)
  matrix products  13.3 us (5%)
  other arithmetic  6.05 us (2%)
    reduce_scatter x1, waiting for transfers between devices, local(): lax.psum_scatter(jnp.dot(table, corr_traces, precision=lax.Precision.HIGH...  131 us
    all_to_all x1, waiting for transfers between devices, local(): lax.all_to_all(outgoing, ('shot', 'cmp'), split_axis=0, concat_axis=0, ti...  49.8 us
    all_to_all x1, waiting for transfers between devices, local(): lax.all_to_all(correlate(lax.all_to_all(outgoing, ('shot', 'cmp'), split_...  10.6 us
    unnamed x132, local copies, waits for them, and re-layouts  9.83 us
    dot_general x1, matrix products, correlate(): jnp.einsum('dbsn,bnl->dbsl', arrived, toeplitz, precision=lax.Precision.H...  8.16 us
    all_to_all x1, starting transfers between devices, local(): lax.all_to_all(markers, ('shot', 'cmp'), split_axis=0, concat_axis=0, til...  7.3 us
    all_to_all x1, starting transfers between devices, local(): lax.all_to_all(outgoing, ('shot', 'cmp'), split_axis=0, concat_axis=0, ti...  6.01 us
  transfers between devices with their start and end apart: 4, of which 3 were waited for; matrix products, arithmetic and copies ran while one was open for 5% of the time, Pallas kernels for 0%

commit v1 on v0

v1 whole, which is shorter than its diff:
```python
import functools

import jax
import jax.numpy as jnp
from jax import lax
from jax.experimental import pallas as pl
from jax.experimental.pallas import tpu as pltpu
from jax.sharding import PartitionSpec as P

LAGS = 128
MAXOFF = 64
SHOT_DEV = 8
RECV_DEV = 16
LANES = 128
CORES = 2
MESH = pl.DeviceIdType.MESH
VMEM_BYTES = 48 * 1024 * 1024


def vmem():
    return pl.BlockSpec(memory_space=pltpu.VMEM)


def halves(value):
    high = value.astype(jnp.bfloat16)
    low = (value - high.astype(jnp.float32)).astype(jnp.bfloat16)
    return high, low


def dot2(table, value, dims):
    high, low = halves(value)
    args = dict(dimension_numbers=(dims, ((), ())), preferred_element_type=jnp.float32)
    return lax.dot_general(table, high, **args) + lax.dot_general(table, low, **args)


def moveout_kernel(bins_count, traces_ref, offsets_ref, bins_ref, band_ref, sums_ref, turned_ref, corrected):
    rows, samples = traces_ref.shape
    taps = band_ref.shape[0]
    width = samples + LANES
    group = 32
    shifts = jnp.transpose(jnp.broadcast_to(offsets_ref[...], (LANES, rows)))
    turned_ref[...] = jnp.zeros_like(turned_ref)
    corrected[:, samples:] = jnp.ones((rows, LANES), jnp.float32)
    for start in range(0, rows, group):
        block = slice(start, start + group)
        current = jnp.concatenate([traces_ref[block, :], jnp.zeros((group, LANES), jnp.float32)], axis=1)
        shift = shifts[block, :]
        for level in range(MAXOFF.bit_length()):
            moved = pltpu.roll(current, width - (1 << level), 1)
            chosen = jnp.concatenate([(shift >> level) & 1] * (width // LANES), axis=1) == 1
            current = jnp.where(chosen, moved, current)
        total = jnp.zeros((group, samples), jnp.float32)
        for tap in range(taps):
            moved = current if tap == 0 else pltpu.roll(current, width - tap, 1)
            total = total + band_ref[tap : tap + 1, :] * moved[:, :samples]
        corrected[block, :samples] = total
    table = (
        bins_ref[...] == lax.broadcasted_iota(jnp.int32, (rows, bins_count), 1)
    ).astype(jnp.float32)
    table = jnp.transpose(table).astype(jnp.bfloat16)
    sums_ref[...] = dot2(table, corrected[...], ((1,), (0,)))
    turned_ref[...] = jnp.transpose(corrected[:, :samples])


def moveout(traces, offsets, cmp_bin, band, bins_count):
    rows, samples = traces.shape
    return pl.pallas_call(
        functools.partial(moveout_kernel, bins_count),
        out_shape=(
            jax.ShapeDtypeStruct((bins_count, samples + LANES), jnp.float32),
            jax.ShapeDtypeStruct((samples, rows), jnp.float32),
        ),
        in_specs=[vmem()] * 4,
        out_specs=(vmem(), vmem()),
        scratch_shapes=[pltpu.VMEM((rows, samples + LANES), jnp.float32)],
        compiler_params=pltpu.CompilerParams(vmem_limit_bytes=VMEM_BYTES),
        name="moveout_sums",
    )(traces, offsets[None, :], cmp_bin, band)


def place(sizes):
    y_size, x_size, z_size = sizes
    shot, cmp = lax.axis_index("shot"), lax.axis_index("cmp")
    return shot % CORES, shot // CORES, cmp % x_size, cmp // x_size


def device(sizes, core, y, x, z):
    return (y * CORES + core, z * sizes[1] + x)


def greet(sizes):
    y_size, x_size, z_size = sizes
    core, y, x, z = place(sizes)
    peers = [device(sizes, 1 - core, y, x, z)]
    peers += [device(sizes, core, (y + k) % y_size, x, z) for k in range(1, y_size)]
    peers += [device(sizes, core, y, (x + k) % x_size, z) for k in range(1, x_size)]
    peers += [device(sizes, core, y, x, (z + k) % z_size) for k in range(1, z_size)]
    barrier = pltpu.get_barrier_semaphore()
    for peer in peers:
        pl.semaphore_signal(barrier, inc=1, device_id=peer, device_id_type=MESH)
    pl.semaphore_wait(barrier, len(peers))


class Sender:
    def __init__(self, send_sems, recv_sems):
        self.send_sems, self.recv_sems, self.used = send_sems, recv_sems, 0

    def start(self, source, target, peer):
        copy = pltpu.make_async_remote_copy(
            src_ref=source,
            dst_ref=target,
            send_sem=self.send_sems.at[self.used],
            recv_sem=self.recv_sems.at[self.used],
            device_id=peer,
            device_id_type=MESH,
        )
        self.used += 1
        copy.start()
        return copy


def scatter_sums(sizes, cut, sender, sums, got_core, acc, got_y, got_x, acc_y, acc_x, got_yx, got_xy, acc_z, got_z):
    y_size, x_size, z_size = sizes
    core, y, x, z = place(sizes)
    lo, hi = pl.ds(0, cut), pl.ds(cut, sums.shape[-1] - cut)
    y_peer = lambda k: device(sizes, core, (y + k) % y_size, x, z)
    x_peer = lambda k: device(sizes, core, y, (x + k) % x_size, z)
    z_peer = lambda k: device(sizes, core, y, x, (z + k) % z_size)
    pending = []

    first = sender.start(sums.at[1 - core], got_core, device(sizes, 1 - core, y, x, z))
    pending.append(first)
    first.wait_recv()
    acc[...] = sums[core] + got_core[...]

    ys = [sender.start(acc.at[(y + k) % y_size, :, :, :, lo], got_y.at[k - 1], y_peer(k)) for k in range(1, y_size)]
    xs = [sender.start(acc.at[:, (x + k) % x_size, :, :, hi], got_x.at[k - 1], x_peer(k)) for k in range(1, x_size)]
    pending += ys + xs
    total = acc[y, :, :, :, :cut]
    for k, copy in enumerate(ys):
        copy.wait_recv()
        total = total + got_y[k]
    acc_y[...] = total
    yxs = [sender.start(acc_y.at[(x + k) % x_size], got_yx.at[k - 1], x_peer(k)) for k in range(1, x_size)]
    total = acc[:, x, :, :, cut:]
    for k, copy in enumerate(xs):
        copy.wait_recv()
        total = total + got_x[k]
    acc_x[...] = total
    xys = [sender.start(acc_x.at[(y + k) % y_size], got_xy.at[k - 1], y_peer(k)) for k in range(1, y_size)]
    pending += yxs + xys
    total = acc_y[x]
    for k, copy in enumerate(yxs):
        copy.wait_recv()
        total = total + got_yx[k]
    acc_z[:, :, :cut] = total
    total = acc_x[y]
    for k, copy in enumerate(xys):
        copy.wait_recv()
        total = total + got_xy[k]
    acc_z[:, :, cut:] = total
    zs = [sender.start(acc_z.at[(z + k) % z_size], got_z.at[k - 1], z_peer(k)) for k in range(1, z_size)]
    pending += zs
    total = acc_z[z]
    for k, copy in enumerate(zs):
        copy.wait_recv()
        total = total + got_z[k]
    return total, pending


def scatter_scratch(sizes, rows, width, cut):
    y_size, x_size, z_size = sizes
    shapes = [
        (y_size, x_size, z_size, rows, width),
        (y_size, x_size, z_size, rows, width),
        (y_size - 1, x_size, z_size, rows, cut),
        (x_size - 1, y_size, z_size, rows, width - cut),
        (x_size, z_size, rows, cut),
        (y_size, z_size, rows, width - cut),
        (x_size - 1, z_size, rows, cut),
        (y_size - 1, z_size, rows, width - cut),
        (z_size, rows, width),
        (z_size - 1, rows, width),
    ]
    return [pltpu.VMEM(shape, jnp.float32) for shape in shapes]


def scatter_copies(sizes):
    return 1 + 2 * (sizes[0] - 1) + 2 * (sizes[1] - 1) + sizes[2] - 1


def pilot_kernel(sizes, cut, sums, pilots, send_sems, recv_sems, *scratch):
    y_size, x_size, z_size = sizes
    core, y, x, z = place(sizes)
    samples = pilots.shape[-1]
    greet(sizes)
    sender = Sender(send_sems, recv_sems)
    total, pending = scatter_sums(sizes, cut, sender, sums, *scratch)
    fold = jnp.concatenate([total[:, samples:]] * (samples // LANES), axis=1)
    pilots[core, y, x, z] = total[:, :samples] / fold

    lo, hi = pl.ds(0, cut), pl.ds(cut, samples - cut)
    other = device(sizes, 1 - core, y, x, z)
    y_peer = lambda k: device(sizes, core, (y + k) % y_size, x, z)
    x_peer = lambda k: device(sizes, core, y, (x + k) % x_size, z)

    def send(view, peer):
        return sender.start(view, view, peer)

    zs = [send(pilots.at[core, y, x, z], device(sizes, core, y, x, (z + k) % z_size)) for k in range(1, z_size)]
    for copy in zs:
        copy.wait_recv()
    own_lo, own_hi = pilots.at[core, y, x, :, :, lo], pilots.at[core, y, x, :, :, hi]
    ys = [send(own_lo, y_peer(k)) for k in range(1, y_size)]
    xs = [send(own_hi, x_peer(k)) for k in range(1, x_size)]
    across = [send(pilots.at[core, y, x], other)]
    for copy in ys:
        copy.wait_recv()
    yxs = [send(pilots.at[core, :, x, :, :, lo], x_peer(k)) for k in range(1, x_size)]
    for copy in xs:
        copy.wait_recv()
    xys = [send(pilots.at[core, y, :, :, :, hi], y_peer(k)) for k in range(1, y_size)]
    for k in range(1, y_size):
        across.append(send(pilots.at[core, (y + k) % y_size, x, :, :, lo], other))
    for k in range(1, x_size):
        across.append(send(pilots.at[core, y, (x + k) % x_size, :, :, hi], other))
    for k, copy in enumerate(yxs, 1):
        copy.wait_recv()
        across.append(send(pilots.at[core, :, (x + k) % x_size, :, :, lo], other))
    for k, copy in enumerate(xys, 1):
        copy.wait_recv()
        across.append(send(pilots.at[core, (y + k) % y_size, :, :, :, hi], other))
    for copy in across:
        copy.wait_recv()
    for copy in pending + zs + ys + xs + yxs + xys + across:
        copy.wait_send()


def share_pilots(sums, sizes, samples):
    y_size, x_size, z_size = sizes
    cut = samples // 2
    blocks = (CORES, y_size, x_size, z_size)
    rows = sums.shape[0] // (CORES * y_size * x_size * z_size)
    width = sums.shape[1]
    copies = scatter_copies(sizes) + (z_size - 1) + 4 * (y_size - 1) + 4 * (x_size - 1) + 1
    pilots = pl.pallas_call(
        functools.partial(pilot_kernel, sizes, cut),
        out_shape=jax.ShapeDtypeStruct(blocks + (rows, samples), jnp.float32),
        in_specs=[vmem()],
        out_specs=vmem(),
        scratch_shapes=[pltpu.SemaphoreType.DMA((copies,))] * 2 + scatter_scratch(sizes, rows, width, cut),
        compiler_params=pltpu.CompilerParams(
            collective_id=0, has_side_effects=True, vmem_limit_bytes=VMEM_BYTES
        ),
        name="share_pilots",
    )(sums.reshape(blocks + (rows, width)))
    return pilots.reshape(sums.shape[0], samples)


def correlate_kernel(turned_ref, pilots_ref, bins_ref, slots_ref, receivers_ref, shot_ref, recv_ref, ahead, moved, parts, corr):
    samples, rows = turned_ref.shape
    bins_count = pilots_ref.shape[0]
    half = LAGS // 2
    span = moved.shape[0]
    table = (
        bins_ref[...] == lax.broadcasted_iota(jnp.int32, (rows, bins_count), 1)
    ).astype(jnp.bfloat16)
    gathered = dot2(table, pilots_ref[...], ((1,), (0,)))
    ahead[:half, :] = jnp.zeros((half, rows), jnp.float32)
    ahead[half : half + samples, :] = jnp.transpose(gathered)
    ahead[half + samples :, :] = jnp.zeros((ahead.shape[0] - half - samples, rows), jnp.float32)
    lags = LAGS // 8
    steps = 4
    for residue in range(8):
        source = ahead if residue == 0 else moved
        if residue > 0:
            moved[...] = ahead[residue : residue + span, :]
        for lane in range(0, rows, LANES):
            columns = slice(lane, lane + LANES)

            def step(index, totals):
                base = pl.multiple_of(index * (8 * steps), 8 * steps)
                signal = [turned_ref[pl.ds(base + 8 * k, 8), columns] for k in range(steps)]
                pilot = [source[pl.ds(base + 8 * k, 8), columns] for k in range(lags + steps - 1)]
                totals = list(totals)
                for lag in range(lags):
                    terms = [signal[k] * pilot[k + lag] for k in range(steps)]
                    totals[lag] = totals[lag] + ((terms[0] + terms[1]) + (terms[2] + terms[3]))
                return tuple(totals)

            zero = jnp.zeros((8, LANES), jnp.float32)
            totals = lax.fori_loop(0, samples // (8 * steps), step, (zero,) * lags)
            for lag in range(lags):
                parts[8 * lag + residue, :, columns] = totals[lag]
    corr[...] = jnp.sum(parts[...], axis=1) * (1.0 / samples)
    high, low = halves(corr[...])
    for ids_ref, out_ref in ((slots_ref, shot_ref), (receivers_ref, recv_ref)):
        count = out_ref.shape[0]
        ids = (ids_ref[...] == lax.broadcasted_iota(jnp.int32, (count, rows), 0)).astype(jnp.bfloat16)
        args = dict(dimension_numbers=(((1,), (1,)), ((), ())), preferred_element_type=jnp.float32)
        out_ref[...] = lax.dot_general(ids, high, **args) + lax.dot_general(ids, low, **args)


def correlate(turned, pilots, cmp_bin, shot_slot, receivers, receivers_count):
    samples, rows = turned.shape
    return pl.pallas_call(
        correlate_kernel,
        out_shape=(
            jax.ShapeDtypeStruct((SHOT_DEV, LAGS), jnp.float32),
            jax.ShapeDtypeStruct((receivers_count, LAGS), jnp.float32),
        ),
        in_specs=[vmem()] * 5,
        out_specs=(vmem(), vmem()),
        scratch_shapes=[
            pltpu.VMEM((samples + LAGS, rows), jnp.float32),
            pltpu.VMEM((samples + LAGS - 8, rows), jnp.float32),
            pltpu.VMEM((LAGS, 8, rows), jnp.float32),
            pltpu.VMEM((LAGS, rows), jnp.float32),
        ],
        compiler_params=pltpu.CompilerParams(vmem_limit_bytes=VMEM_BYTES),
        name="correlate_sums",
    )(turned, pilots, cmp_bin, shot_slot[None, :], receivers[None, :])


def local(sizes, bins_count, traces, offsets, cmp_bin, shot_slot, receiver_id, band):
    samples = traces.shape[1]
    devices = lax.axis_size(("shot", "cmp"))
    sums, turned = moveout(traces, offsets, cmp_bin, band, bins_count)
    pilots = share_pilots(sums, sizes, samples)
    shot_corr, partial = correlate(turned, pilots, cmp_bin, shot_slot, receiver_id, RECV_DEV * devices)
    parts = lax.all_to_all(
        partial.reshape(devices, RECV_DEV, LAGS), ("shot", "cmp"), split_axis=0, concat_axis=0, tiled=True
    )
    return shot_corr, jnp.sum(parts, axis=0)


def solution(mesh):
    shot_size, cmp_size = mesh.shape["shot"], mesh.shape["cmp"]
    z_size = 4 if cmp_size % 4 == 0 else 1
    sizes = (shot_size // CORES, cmp_size // z_size, z_size)
    placed = (
        P(("shot", "cmp"), None),
        P(("shot", "cmp")),
        P(("shot", "cmp"), None),
        P(("shot", "cmp")),
        P(("shot", "cmp")),
        P(),
    )

    def whole(traces, offsets, cmp_bin, shot_slot, receiver_id, band):
        bins_count = traces.shape[0] // (shot_size * cmp_size)
        return jax.shard_map(
            functools.partial(local, sizes, bins_count),
            mesh=mesh,
            in_specs=placed,
            out_specs=(P(("shot", "cmp"), None), P(("shot", "cmp"), None)),
            check_vma=False,
        )(traces, offsets, cmp_bin, shot_slot, receiver_id, band)

    return whole
```

time: 261 us -> 76.9 us (0.29)
  waiting for transfers between devices: 191 us -> 0 us
  Pallas kernels: 0 us -> 58.3 us
  starting transfers between devices: 16.6 us -> 0 us
  local copies, waits for them, and re-layouts: 19 us -> 3.48 us
  between operations: 14.3 us -> 0.7 us
  blocking collectives: 0 us -> 13.5 us
  matrix products: 13.3 us -> 0 us
  other arithmetic: 6.05 us -> 0.63 us
    reduce_scatter x1 -> x0, waiting for transfers between devices: 131 us -> none  [local(): lax.psum_scatter(jnp.dot(table, corr_traces, precision=lax.Precision.HIGH...]
    all_to_all x3 -> x0, waiting for transfers between devices: 60.4 us -> none  [the longest x1 49.8 us: local(): lax.all_to_all(outgoing, ('shot', 'cmp'), split_axis=0, concat_axis=0, ti...]
    pallas_call x0 -> x3, Pallas kernels: none -> 58.3 us  [the longest x1 34.7 us: share_pilots(): pl.pallas_call(functools.partial(pilot_kernel, sizes, cut), out_shape=jax...]
    all_to_all x3 -> x0, starting transfers between devices: 16.6 us -> none  [the longest x1 7.3 us: local(): lax.all_to_all(markers, ('shot', 'cmp'), split_axis=0, concat_axis=0, til...]
    all_to_all x0 -> x1, blocking collectives: none -> 13.5 us  [local(): lax.all_to_all(partial.reshape(devices, RECV_DEV, LAGS), ('shot', 'cmp'),...]
    dot_general x5 -> x0, matrix products: 13.3 us -> none  [the longest x1 8.16 us: correlate(): jnp.einsum('dbsn,bnl->dbsl', arrived, toeplitz, precision=lax.Precision.H...]
    unnamed x132 -> x11, local copies, waits for them, and re-layouts: 9.83 us -> 3.48 us
    slice x8 -> x0, local copies, waits for them, and re-layouts: 4.87 us -> none  [the longest x7 3.79 us: moveout(): moved = jnp.pad(current[:, step:], ((0, 0), (0, step)))]
  transfers between devices with their start and end apart: 4 -> 0, of which waited for: 3 -> 0; matrix products, arithmetic and copies ran while one was open for 5% -> 0% of each run, Pallas kernels for 0% -> 0%
where the time goes in v1:
time: 76.9 us; the launch traced here: 76.6 us
  Pallas kernels  58.3 us (76%)
  blocking collectives  13.5 us (18%)
  local copies, waits for them, and re-layouts  3.48 us (5%)
    pallas_call x1, Pallas kernels, share_pilots(): pl.pallas_call(functools.partial(pilot_kernel, sizes, cut), out_shape=jax...  34.7 us
    pallas_call x1, Pallas kernels, correlate(): pl.pallas_call(correlate_kernel, out_shape=(jax.ShapeDtypeStruct((SHOT_DE...  16.8 us
    all_to_all x1, blocking collectives, local(): lax.all_to_all(partial.reshape(devices, RECV_DEV, LAGS), ('shot', 'cmp'),...  13.5 us
    pallas_call x1, Pallas kernels, moveout(): pl.pallas_call(functools.partial(moveout_kernel, bins_count), out_shape=(...  6.87 us
    unnamed x11, local copies, waits for them, and re-layouts  3.48 us

profile of v1, /device:TPU:0, one launch (start us, length us, event | category | flops | bytes accessed | tf_op | source)
XLA Modules:
  0.0 76.6 jit_solution(11569875877252870699)
XLA Ops:
  0.6 0.8 %copy.8.bins_ref = s32[256,1]{1,0:T(8,128)S(1)} copy(s32[256,1]{0,1:T(1,128)} %param.8) | data formatting | bytes 2048 | tf_op args[2]
  1.4 0.0 copy-start
  1.5 1.2 %copy-done = f32[256,1024]{1,0:T(8,128)S(1)} copy-done((f32[256,1024]{1,0:T(8,128)S(1)}, f32[256,1024]{1,0:T(8,128)}, u32[]{:S(2)}) %copy-start) | copy-done | bytes 1048600
  2.7 0.0 copy-start.1
  2.7 0.8 copy-done.1
  3.4 0.0 copy-start.4
  3.4 0.7 copy-done.4
  4.1 6.9 %moveout_sums.1 = (f32[256,1152]{1,0:T(8,128)S(1)}, f32[1024,256]{1,0:T(8,128)S(1)}) custom-call(f32[256,1024]{1,0:T(8,128)S(1)} %copy-done, s32[1,256]{1,0:T(1,128)S(1)} %bitcast.11, s32[256,1]{1,0:T(8,128)S(1)} %copy.8.bins_ref, f32[8,1024]{1,0:T(8,128)S(1)} %copy-done.1), custom_call_target="tpu_custom_call" | custom-call | tf_op jit(solution)/shard_map/moveout_sums/pallas_call | solution.py:67
  11.0 0.0 copy-start.2
  11.0 0.0 copy-start.3
  11.0 34.7 %share_pilots.1 = f32[2,2,2,4,8,1024]{5,4,3,2,1,0:T(8,128)S(1)} custom-call(f32[2,2,2,4,8,1152]{5,4,3,2,1,0:T(8,128)S(1)} %bitcast.7), custom_call_target="tpu_custom_call" | custom-call | tf_op jit(solution)/shard_map/share_pilots/pallas_call | solution.py:246
  45.7 0.0 copy-done.2
  45.7 0.0 copy-done.3
  45.7 16.8 %correlate_sums.1 = (f32[8,128]{1,0:T(8,128)}, f32[512,128]{1,0:T(8,128)S(1)}) custom-call(f32[1024,256]{1,0:T(8,128)S(1)} %get-tuple-element.6.turned_ref, f32[256,1024]{1,0:T(8,128)S(1)} %bitcast.6, s32[256,1]{1,0:T(8,128)S(1)} %copy.8.bins_ref, s32[1,256]{1,0:T(1,128)S(1)} %bitcast.9, s32[1,256]{1,0:T(1,128)S(1)} %bitcast.10), custom_call_target="tpu_custom_call" | custom-call | tf_op jit(solution)/shard_map/correlate_sums/pallas_call | solution.py:306
  62.5 13.5 %all_to_all.5 = f32[32,16,128]{2,1,0:T(8,128)S(1)} all-to-all(f32[32,16,128]{2,1,0:T(8,128)S(1)} %bitcast.8), channel_id=1, replica_groups=mesh['shot'=4,'cmp'=8] {'shot','cmp'}, dimensions={0} | all-to-all | bytes 524288 | tf_op jit(solution)/shard_map/all_to_all | solution.py:331
  76.0 0.6 reduce_sum.9
Async XLA Ops:
  1.4 1.2 %copy-start = (f32[256,1024]{1,0:T(8,128)S(1)}, f32[256,1024]{1,0:T(8,128)}, u32[]{:S(2)}) copy-start(f32[256,1024]{1,0:T(8,128)} %traces_ref.1) | copy-start | bytes 3145732
  2.7 0.8 copy-start.1
  3.4 0.7 copy-start.4
  11.0 34.7 %copy-start.2 = (s32[256]{0:T(256)S(1)}, s32[256]{0:T(256)}, u32[]{:S(2)}) copy-start(s32[256]{0:T(256)} %param.9) | copy-start | bytes 3076
  11.0 34.7 %copy-start.3 = (s32[256]{0:T(256)S(1)}, s32[256]{0:T(256)}, u32[]{:S(2)}) copy-start(s32[256]{0:T(256)} %param.10) | copy-start | bytes 3076

commit v2 on v0

v2 whole, which is shorter than its diff:
```python
import functools

import jax
import jax.numpy as jnp
from jax import lax
from jax.experimental import pallas as pl
from jax.experimental.pallas import tpu as pltpu
from jax.sharding import PartitionSpec as P

LAGS = 128
MAXOFF = 64
SHOT_DEV = 8
RECV_DEV = 16
LANES = 128
CORES = 2
CHUNKS = 4
GROUP = 32
MESH = pl.DeviceIdType.MESH
VMEM_BYTES = 56 * 1024 * 1024


def halves(value):
    high = value.astype(jnp.bfloat16)
    low = (value - high.astype(jnp.float32)).astype(jnp.bfloat16)
    return high, low


def dot2(table, value, dims):
    high, low = halves(value)
    args = dict(dimension_numbers=(dims, ((), ())), preferred_element_type=jnp.float32)
    return lax.dot_general(table, high, **args) + lax.dot_general(table, low, **args)


def log2(size):
    return size.bit_length() - 1


class Sender:
    def __init__(self, send_sems, recv_sems):
        self.send_sems, self.recv_sems, self.copies = send_sems, recv_sems, []

    def start(self, source, target, peer):
        copy = pltpu.make_async_remote_copy(
            src_ref=source,
            dst_ref=target,
            send_sem=self.send_sems.at[len(self.copies)],
            recv_sem=self.recv_sems.at[len(self.copies)],
            device_id=peer,
            device_id_type=MESH,
        )
        self.copies.append(copy)
        copy.start()
        return copy


def copies_count(plane, z_size):
    scatter = 1 + (plane - 1) + (z_size - 1)
    return CHUNKS * (2 * scatter + plane - 1) + scatter


def kernel(
    sizes,
    traces_ref, offsets_ref, bins_ref, slots_ref, receivers_ref, band_ref,
    shot_ref, recv_ref,
    traces, corrected, table_t, table, shifts, padded, moved, ahead, parts, fold,
    sums, got_core, acc, got_plane, acc_z, got_z, pilots,
    rsums, rgot_core, racc, rgot_plane, racc_z, rgot_z,
    load_sems, send_sems, recv_sems,
):
    y_size, x_size, z_size = sizes
    plane = y_size * x_size
    shot, cmp = lax.axis_index("shot"), lax.axis_index("cmp")
    core, y, x, z = shot % CORES, shot // CORES, cmp % x_size, cmp // x_size
    q = y * x_size + x
    rows, samples = traces_ref.shape
    bins_count = rows
    chunk = samples // CHUNKS
    taps = band_ref.shape[0]
    held = sums.shape[-2]
    half = LAGS // 2

    def device(core, q, z):
        return ((q // x_size) * CORES + core, z * x_size + q % x_size)

    other = device(1 - core, q, z)
    plane_peers = [device(core, (q + k) % plane, z) for k in range(1, plane)]
    z_peers = [device(core, q, (z + k) % z_size) for k in range(1, z_size)]

    loads = []
    for k in range(CHUNKS):
        columns = pl.ds(k * chunk, chunk)
        loads.append(pltpu.make_async_copy(traces_ref.at[:, columns], traces.at[:, columns], load_sems.at[k]))
        loads[-1].start()
    barrier = pltpu.get_barrier_semaphore()
    peers = [other] + plane_peers + z_peers
    for peer in peers:
        pl.semaphore_signal(barrier, inc=1, device_id=peer, device_id_type=MESH)

    sender = Sender(send_sems, recv_sems)
    shifts[...] = jnp.transpose(jnp.broadcast_to(offsets_ref[...], (LANES, rows)))
    named = (bins_ref[...] == lax.broadcasted_iota(jnp.int32, (bins_count, rows), 0)).astype(jnp.float32)
    table_t[...] = named.astype(jnp.bfloat16)
    table[...] = jnp.transpose(named).astype(jnp.bfloat16)
    traces[:, samples:] = jnp.zeros((rows, LANES), jnp.float32)
    corrected[:, chunk:] = jnp.ones((rows, LANES), jnp.float32)
    padded[:half, :] = jnp.zeros((half, rows), jnp.float32)
    padded[half + samples :, :] = jnp.zeros((half, rows), jnp.float32)

    def width_of(k):
        return chunk + LANES if k == 0 else chunk

    def correct(k):
        first = k * chunk
        loads[k].wait() if k == 0 else None
        if k + 1 < CHUNKS:
            loads[k + 1].wait()
        span = chunk + LANES

        def group(index, carry):
            block = pl.ds(pl.multiple_of(index * GROUP, GROUP), GROUP)
            current = traces[block, first : first + span]
            shift = shifts[block, :]
            for level in range(MAXOFF.bit_length()):
                turned = pltpu.roll(current, span - (1 << level), 1)
                chosen = jnp.concatenate([(shift >> level) & 1] * (span // LANES), axis=1) == 1
                current = jnp.where(chosen, turned, current)
            total = jnp.zeros((GROUP, chunk), jnp.float32)
            for tap in range(taps):
                turned = current if tap == 0 else pltpu.roll(current, span - tap, 1)
                total = total + band_ref[tap : tap + 1, first : first + chunk] * turned[:, :chunk]
            corrected[block, :chunk] = total
            return carry

        lax.fori_loop(0, rows // GROUP, group, 0)
        width = width_of(k)
        result = dot2(table_t[...], corrected[:, :width], ((1,), (0,)))
        if held % 8 == 0:
            sums[k, :, :, :, :, :width] = result.reshape(CORES, plane, z_size, held, width)
        else:
            for block in range(CORES * plane * z_size):
                c_of, rest = divmod(block, plane * z_size)
                sums[k, c_of, rest // z_size, rest % z_size, :, :width] = result[block * held : (block + 1) * held]
        padded[half + first : half + first + chunk, :] = jnp.transpose(corrected[:, :chunk])

    def scatter_core(k):
        lanes = pl.ds(0, width_of(k))
        return [sender.start(sums.at[k, 1 - core, :, :, :, lanes], got_core.at[k, :, :, :, lanes], other)]

    def scatter_plane(k, waits):
        width = width_of(k)
        lanes = pl.ds(0, width)
        waits[0].wait_recv()
        acc[k, :, :, :, :width] = sums[k, core, :, :, :, :width] + got_core[k, :, :, :, :width]
        return [
            sender.start(acc.at[k, (q + j) % plane, :, :, lanes], got_plane.at[k, j - 1, :, :, lanes], plane_peers[j - 1])
            for j in range(1, plane)
        ]

    def scatter_z(k, waits):
        width = width_of(k)
        lanes = pl.ds(0, width)
        total = acc[k, q, :, :, :width]
        for j, copy in enumerate(waits):
            copy.wait_recv()
            total = total + got_plane[k, j, :, :, :width]
        acc_z[k, :, :, :width] = total
        return [
            sender.start(acc_z.at[k, (z + j) % z_size, :, lanes], got_z.at[k, j - 1, :, lanes], z_peers[j - 1])
            for j in range(1, z_size)
        ]

    def gather_z(k, waits):
        width = width_of(k)
        total = acc_z[k, z, :, :width]
        for j, copy in enumerate(waits):
            copy.wait_recv()
            total = total + got_z[k, j, :, :width]
        if k == 0:
            fold[...] = total[:, chunk:]
        pilots[k, core, q, z] = total[:, :chunk] / jnp.concatenate([fold[...]] * (chunk // LANES), axis=1)
        own = pilots.at[k, core, q, z]
        return [sender.start(own, own, peer) for peer in z_peers]

    def gather_plane(k, waits):
        for copy in waits:
            copy.wait_recv()
        own = pilots.at[k, core, q]
        return [sender.start(own, own, peer) for peer in plane_peers] + [sender.start(own, own, other)]

    def gather_core(k, waits):
        across = [waits[-1]]
        for j, copy in enumerate(waits[:-1], 1):
            copy.wait_recv()
            came = pilots.at[k, core, (q + plane - j) % plane]
            across.append(sender.start(came, came, other))
        return across

    def correlate(k, waits):
        for copy in waits:
            copy.wait_recv()
        if held % 8 == 0:
            pilot = pilots[k].reshape(bins_count, chunk)
        else:
            pilot = jnp.concatenate(
                [
                    pilots[k, n // (plane * z_size), n // z_size % plane, n % z_size]
                    for n in range(CORES * plane * z_size)
                ],
                axis=0,
            )
        ahead[...] = jnp.transpose(dot2(table[...], pilot, ((1,), (0,))))
        lags = LAGS // 8
        steps = 4

        def residue(index, carry):
            for lane in range(0, rows, LANES):
                columns = slice(lane, lane + LANES)

                def step(index_in, totals):
                    base = pl.multiple_of(index_in * (8 * steps), 8 * steps)
                    signal = [ahead[pl.ds(base + 8 * i, 8), columns] for i in range(steps)]
                    shifted = [
                        moved[index, pl.ds(k * chunk + base + 8 * i, 8), columns] for i in range(lags + steps - 1)
                    ]
                    totals = list(totals)
                    for lag in range(lags):
                        terms = [signal[i] * shifted[i + lag] for i in range(steps)]
                        totals[lag] = totals[lag] + ((terms[0] + terms[1]) + (terms[2] + terms[3]))
                    return tuple(totals)

                zero = jnp.zeros((8, LANES), jnp.float32)
                before = tuple(
                    zero if k == 0 else parts[lags - 1 - lag, 7 - index, :, columns] for lag in range(lags)
                )
                totals = lax.fori_loop(0, chunk // (8 * steps), step, before)
                for lag in range(lags):
                    parts[lags - 1 - lag, 7 - index, :, columns] = totals[lag]
            return carry

        lax.fori_loop(0, 8, residue, 0)

    def shift_copies(index):
        moved[index] = padded[index + 1 : index + 1 + moved.shape[1], :]

    stages = [scatter_plane, scatter_z, gather_z, gather_plane, gather_core, correlate]
    waits = [None] * CHUNKS
    fillers = list(range(8))
    for turn in range(CHUNKS + len(stages)):
        if turn < CHUNKS:
            correct(turn)
            if turn == 0:
                pl.semaphore_wait(barrier, len(peers))
            waits[turn] = scatter_core(turn)
        for k in range(CHUNKS):
            stage = turn - k - 1
            if 0 <= stage < len(stages) - 1:
                waits[k] = stages[stage](k, waits[k])
        if turn >= CHUNKS - 1:
            for _ in range(4):
                if fillers:
                    shift_copies(fillers.pop())
        k = turn - len(stages)
        if 0 <= k < CHUNKS:
            while fillers:
                shift_copies(fillers.pop())
            correlate(k, waits[k])

    corr = (jnp.sum(parts[...], axis=2) * (1.0 / samples)).reshape(LAGS, rows)
    high, low = halves(corr)

    def tabled(ids, count):
        args = dict(dimension_numbers=(((1,), (1,)), ((), ())), preferred_element_type=jnp.float32)
        chosen = (ids == lax.broadcasted_iota(jnp.int32, (count, rows), 0)).astype(jnp.bfloat16)
        return lax.dot_general(chosen, high, **args) + lax.dot_general(chosen, low, **args)

    ids = receivers_ref[...]
    within = ids & (RECV_DEV - 1)
    owner = ids >> log2(RECV_DEV)
    owner_x = owner & (x_size - 1)
    owner_z = (owner >> log2(x_size)) & (z_size - 1)
    owner_core = (owner >> log2(x_size * z_size)) & 1
    owner_y = owner >> log2(x_size * z_size * CORES)
    block = ((owner_core * y_size + owner_y) * x_size + owner_x) * z_size + owner_z
    rsums[...] = tabled(block * RECV_DEV + within, CORES * plane * z_size * RECV_DEV).reshape(rsums.shape)
    first = sender.start(rsums.at[1 - core], rgot_core, other)
    shot_ref[...] = tabled(slots_ref[...], SHOT_DEV)
    first.wait_recv()
    racc[...] = rsums[core] + rgot_core[...]
    waiting = [
        sender.start(racc.at[(q + j) % plane], rgot_plane.at[j - 1], plane_peers[j - 1]) for j in range(1, plane)
    ]
    total = racc[q]
    for j, copy in enumerate(waiting):
        copy.wait_recv()
        total = total + rgot_plane[j]
    racc_z[...] = total
    waiting = [
        sender.start(racc_z.at[(z + j) % z_size], rgot_z.at[j - 1], z_peers[j - 1]) for j in range(1, z_size)
    ]
    total = racc_z[z]
    for j, copy in enumerate(waiting):
        copy.wait_recv()
        total = total + rgot_z[j]
    recv_ref[...] = total
    for copy in sender.copies:
        copy.wait_send()


def local(sizes, traces, offsets, cmp_bin, shot_slot, receiver_id, band):
    rows, samples = traces.shape
    y_size, x_size, z_size = sizes
    plane = y_size * x_size
    held = rows // (CORES * plane * z_size)
    chunk = samples // CHUNKS
    wide = chunk + LANES
    copies = copies_count(plane, z_size)

    def buffer(*shape):
        return pltpu.VMEM(shape, jnp.float32)

    vmem = pl.BlockSpec(memory_space=pltpu.VMEM)
    return pl.pallas_call(
        functools.partial(kernel, sizes),
        out_shape=(
            jax.ShapeDtypeStruct((SHOT_DEV, LAGS), jnp.float32),
            jax.ShapeDtypeStruct((RECV_DEV, LAGS), jnp.float32),
        ),
        in_specs=[pl.BlockSpec(memory_space=pl.ANY)] + [vmem] * 5,
        out_specs=(vmem, vmem),
        scratch_shapes=[
            buffer(rows, samples + LANES),
            buffer(rows, wide),
            pltpu.VMEM((rows, rows), jnp.bfloat16),
            pltpu.VMEM((rows, rows), jnp.bfloat16),
            pltpu.VMEM((rows, LANES), jnp.int32),
            buffer(samples + LAGS, rows),
            buffer(8, samples + LAGS - 8, rows),
            buffer(chunk, rows),
            buffer(LAGS // 8, 8, 8, rows),
            buffer(held, LANES),
            buffer(CHUNKS, CORES, plane, z_size, held, wide),
            buffer(CHUNKS, plane, z_size, held, wide),
            buffer(CHUNKS, plane, z_size, held, wide),
            buffer(CHUNKS, plane - 1, z_size, held, wide),
            buffer(CHUNKS, z_size, held, wide),
            buffer(CHUNKS, z_size - 1, held, wide),
            buffer(CHUNKS, CORES, plane, z_size, held, chunk),
            buffer(CORES, plane, z_size, RECV_DEV, LAGS),
            buffer(plane, z_size, RECV_DEV, LAGS),
            buffer(plane, z_size, RECV_DEV, LAGS),
            buffer(plane - 1, z_size, RECV_DEV, LAGS),
            buffer(z_size, RECV_DEV, LAGS),
            buffer(z_size - 1, RECV_DEV, LAGS),
            pltpu.SemaphoreType.DMA((CHUNKS,)),
            pltpu.SemaphoreType.DMA((copies,)),
            pltpu.SemaphoreType.DMA((copies,)),
        ],
        compiler_params=pltpu.CompilerParams(
            collective_id=0, has_side_effects=True, vmem_limit_bytes=VMEM_BYTES
        ),
        name="residual_statics",
    )(
        traces,
        offsets.reshape(1, rows),
        cmp_bin.reshape(1, rows),
        shot_slot.reshape(1, rows),
        receiver_id.reshape(1, rows),
        band,
    )


def solution(mesh):
    shot_size, cmp_size = mesh.shape["shot"], mesh.shape["cmp"]
    z_size = 4 if cmp_size % 8 == 0 else 2
    sizes = (shot_size // CORES, cmp_size // z_size, z_size)
    placed = (
        P(("shot", "cmp"), None),
        P(("shot", "cmp")),
        P(("shot", "cmp"), None),
        P(("shot", "cmp")),
        P(("shot", "cmp")),
        P(),
    )
    return jax.shard_map(
        functools.partial(local, sizes),
        mesh=mesh,
        in_specs=placed,
        out_specs=(P(("shot", "cmp"), None), P(("shot", "cmp"), None)),
        check_vma=False,
    )
```

time: 261 us -> 76.1 us (0.29)
  waiting for transfers between devices: 191 us -> 0 us
  Pallas kernels: 0 us -> 73.3 us
  local copies, waits for them, and re-layouts: 19 us -> 1.88 us
  starting transfers between devices: 16.6 us -> 0 us
  between operations: 14.3 us -> 0.65 us
  matrix products: 13.3 us -> 0 us
  other arithmetic: 6.05 us -> 0 us
    reduce_scatter x1 -> x0, waiting for transfers between devices: 131 us -> none  [local(): lax.psum_scatter(jnp.dot(table, corr_traces, precision=lax.Precision.HIGH...]
    pallas_call x0 -> x1, Pallas kernels: none -> 73.3 us  [local(): pl.pallas_call(functools.partial(kernel, sizes), out_shape=(jax.ShapeDtyp...]
    all_to_all x3 -> x0, waiting for transfers between devices: 60.4 us -> none  [the longest x1 49.8 us: local(): lax.all_to_all(outgoing, ('shot', 'cmp'), split_axis=0, concat_axis=0, ti...]
    all_to_all x3 -> x0, starting transfers between devices: 16.6 us -> none  [the longest x1 7.3 us: local(): lax.all_to_all(markers, ('shot', 'cmp'), split_axis=0, concat_axis=0, til...]
    dot_general x5 -> x0, matrix products: 13.3 us -> none  [the longest x1 8.16 us: correlate(): jnp.einsum('dbsn,bnl->dbsl', arrived, toeplitz, precision=lax.Precision.H...]
    unnamed x132 -> x4, local copies, waits for them, and re-layouts: 9.83 us -> 1.88 us
    slice x8 -> x0, local copies, waits for them, and re-layouts: 4.87 us -> none  [the longest x7 3.79 us: moveout(): moved = jnp.pad(current[:, step:], ((0, 0), (0, step)))]
    reshape x3 -> x0, local copies, waits for them, and re-layouts: 3.3 us -> none  [the longest x1 2.3 us: local(): outgoing = outgoing.reshape(devices, bins_here, SLOT, samples)]
  transfers between devices with their start and end apart: 4 -> 0, of which waited for: 3 -> 0; matrix products, arithmetic and copies ran while one was open for 5% -> 0% of each run, Pallas kernels for 0% -> 0%
where the time goes in v2:
time: 76.1 us; the launch traced here: 75.8 us
  Pallas kernels  73.3 us (96%)
  local copies, waits for them, and re-layouts  1.88 us (2%)
    pallas_call x1, Pallas kernels, local(): pl.pallas_call(functools.partial(kernel, sizes), out_shape=(jax.ShapeDtyp...  73.3 us
    unnamed x4, local copies, waits for them, and re-layouts  1.88 us

profile of v2, /device:TPU:0, one launch (start us, length us, event | category | flops | bytes accessed | tf_op | source)
XLA Modules:
  0.0 75.8 jit_solution(16366599893846000978)
XLA Ops:
  0.6 73.3 %residual_statics.1 = (f32[8,128]{1,0:T(8,128)}, f32[16,128]{1,0:T(8,128)}) custom-call(f32[256,1024]{1,0:T(8,128)} %traces_ref.1, s32[1,256]{1,0:T(1,128)} %bitcast.4, s32[1,256]{1,0:T(1,128)} %bitcast.5, s32[1,256]{1,0:T(1,128)} %bitcast.6, s32[1,256]{1,0:T(1,128)} %bitcast.7, f32[8,1024]{1,0:T(8,128)} %band_ref.1), custom_call_target="tpu_custom_call" | custom-call | tf_op jit(solution)/shard_map/residual_statics/pallas_call | solution.py:322
  73.9 0.0 copy-start
  73.9 1.3 %copy.10 = f32[8,128]{1,0:T(8,128)} copy(f32[8,128]{1,0:T(8,128)} %get-tuple-element.4) | data formatting | bytes 8192
  75.2 0.0 copy-done
  75.2 0.6 copy.11
Async XLA Ops:
  73.9 1.3 %copy-start = (f32[16,128]{1,0:T(8,128)S(1)}, f32[16,128]{1,0:T(8,128)}, u32[]{:S(2)}) copy-start(f32[16,128]{1,0:T(8,128)} %get-tuple-element.5) | copy-start | bytes 24580

commit v3 on v2

--- a/solution.py
+++ b/solution.py
@@ -15,6 +15,7 @@
 CORES = 2
 CHUNKS = 4
 GROUP = 32
+UNIT = 1
 MESH = pl.DeviceIdType.MESH
 VMEM_BYTES = 56 * 1024 * 1024
 
@@ -117,7 +118,7 @@
         span = chunk + LANES
 
         def group(index, carry):
-            block = pl.ds(pl.multiple_of(index * GROUP, GROUP), GROUP)
+            block = slice(index * GROUP, (index + 1) * GROUP)
             current = traces[block, first : first + span]
             shift = shifts[block, :]
             for level in range(MAXOFF.bit_length()):
@@ -131,7 +132,8 @@
             corrected[block, :chunk] = total
             return carry
 
-        lax.fori_loop(0, rows // GROUP, group, 0)
+        for index in range(rows // GROUP):
+            group(index, 0)
         width = width_of(k)
         result = dot2(table_t[...], corrected[:, :width], ((1,), (0,)))
         if held % 8 == 0:
@@ -195,7 +197,7 @@
             across.append(sender.start(came, came, other))
         return across
 
-    def correlate(k, waits):
+    def arrive(k, waits):
         for copy in waits:
             copy.wait_recv()
         if held % 8 == 0:
@@ -208,9 +210,11 @@
                 ],
                 axis=0,
             )
-        ahead[...] = jnp.transpose(dot2(table[...], pilot, ((1,), (0,))))
+        ahead[k * chunk : (k + 1) * chunk, :] = jnp.transpose(dot2(table[...], pilot, ((1,), (0,))))
+
+    def correlate(first, last):
         lags = LAGS // 8
-        steps = 4
+        steps = 8
 
         def residue(index, carry):
             for lane in range(0, rows, LANES):
@@ -218,31 +222,34 @@
 
                 def step(index_in, totals):
                     base = pl.multiple_of(index_in * (8 * steps), 8 * steps)
-                    signal = [ahead[pl.ds(base + 8 * i, 8), columns] for i in range(steps)]
+                    signal = [ahead[pl.ds(first * chunk + base + 8 * i, 8), columns] for i in range(steps)]
                     shifted = [
-                        moved[index, pl.ds(k * chunk + base + 8 * i, 8), columns] for i in range(lags + steps - 1)
+                        moved[index, pl.ds(first * chunk + base + 8 * i, 8), columns] for i in range(lags + steps - 1)
                     ]
                     totals = list(totals)
                     for lag in range(lags):
                         terms = [signal[i] * shifted[i + lag] for i in range(steps)]
-                        totals[lag] = totals[lag] + ((terms[0] + terms[1]) + (terms[2] + terms[3]))
+                        while len(terms) > 1:
+                            terms = [terms[i] + terms[i + 1] for i in range(0, len(terms), 2)]
+                        totals[lag] = totals[lag] + terms[0]
                     return tuple(totals)
 
                 zero = jnp.zeros((8, LANES), jnp.float32)
                 before = tuple(
-                    zero if k == 0 else parts[lags - 1 - lag, 7 - index, :, columns] for lag in range(lags)
+                    zero if first == 0 else parts[lags - 1 - lag, 7 - index, :, columns] for lag in range(lags)
                 )
-                totals = lax.fori_loop(0, chunk // (8 * steps), step, before)
+                totals = lax.fori_loop(0, (last - first) * chunk // (8 * steps), step, before)
                 for lag in range(lags):
                     parts[lags - 1 - lag, 7 - index, :, columns] = totals[lag]
             return carry
 
-        lax.fori_loop(0, 8, residue, 0)
+        for index in range(8):
+            residue(index, 0)
 
     def shift_copies(index):
         moved[index] = padded[index + 1 : index + 1 + moved.shape[1], :]
 
-    stages = [scatter_plane, scatter_z, gather_z, gather_plane, gather_core, correlate]
+    stages = [scatter_plane, scatter_z, gather_z, gather_plane, gather_core, arrive]
     waits = [None] * CHUNKS
     fillers = list(range(8))
     for turn in range(CHUNKS + len(stages)):
@@ -263,7 +270,9 @@
         if 0 <= k < CHUNKS:
             while fillers:
                 shift_copies(fillers.pop())
-            correlate(k, waits[k])
+            arrive(k, waits[k])
+            if (k + 1) % UNIT == 0:
+                correlate(k + 1 - UNIT, k + 1)
 
     corr = (jnp.sum(parts[...], axis=2) * (1.0 / samples)).reshape(LAGS, rows)
     high, low = halves(corr)
@@ -335,7 +344,7 @@
             pltpu.VMEM((rows, LANES), jnp.int32),
             buffer(samples + LAGS, rows),
             buffer(8, samples + LAGS - 8, rows),
-            buffer(chunk, rows),
+            buffer(samples, rows),
             buffer(LAGS // 8, 8, 8, rows),
             buffer(held, LANES),
             buffer(CHUNKS, CORES, plane, z_size, held, wide),

time: 76.1 us -> 60.2 us (0.79)
  Pallas kernels: 73.3 us -> 57.4 us
    pallas_call x1, Pallas kernels: 73.3 us -> 57.4 us  [local(): pl.pallas_call(functools.partial(kernel, sizes), out_shape=(jax.ShapeDtyp...]
where the time goes in v3:
time: 60.2 us; the launch traced here: 59.9 us
  Pallas kernels  57.4 us (95%)
  local copies, waits for them, and re-layouts  1.88 us (3%)
  between operations  0.65 us (1%)
    pallas_call x1, Pallas kernels, local(): pl.pallas_call(functools.partial(kernel, sizes), out_shape=(jax.ShapeDtyp...  57.4 us
    unnamed x4, local copies, waits for them, and re-layouts  1.88 us

profile of v3, /device:TPU:0, one launch (start us, length us, event | category | flops | bytes accessed | tf_op | source)
XLA Modules:
  0.0 59.9 jit_solution(6108379394695396312)
XLA Ops:
  0.6 57.4 %residual_statics.1 = (f32[8,128]{1,0:T(8,128)}, f32[16,128]{1,0:T(8,128)}) custom-call(f32[256,1024]{1,0:T(8,128)} %traces_ref.1, s32[1,256]{1,0:T(1,128)} %bitcast.4, s32[1,256]{1,0:T(1,128)} %bitcast.5, s32[1,256]{1,0:T(1,128)} %bitcast.6, s32[1,256]{1,0:T(1,128)} %bitcast.7, f32[8,1024]{1,0:T(8,128)} %band_ref.1), custom_call_target="tpu_custom_call" | custom-call | tf_op jit(solution)/shard_map/residual_statics/pallas_call | solution.py:331
  58.0 0.0 copy-start
  58.1 1.3 %copy.10 = f32[8,128]{1,0:T(8,128)} copy(f32[8,128]{1,0:T(8,128)} %get-tuple-element.4) | data formatting | bytes 8192
  59.3 0.0 copy-done
  59.3 0.6 copy.11
Async XLA Ops:
  58.0 1.3 %copy-start = (f32[16,128]{1,0:T(8,128)S(1)}, f32[16,128]{1,0:T(8,128)}, u32[]{:S(2)}) copy-start(f32[16,128]{1,0:T(8,128)} %get-tuple-element.5) | copy-start | bytes 24580
